TPU v7x, 128 devices: a whole 4x4x4 slice. The times are simulated.
128 devices in a mesh: prow: 8 (over x, core), pcol: 16 (over z, y).
Axes of the slice: x: 4, y: 4, z: 4, core: 2. Of those that a mesh axis runs over, the one named last changes fastest.
Arguments:
- matrix: float32 [8, 16, 768, 384], P('prow', 'pcol'), may hold values from -6 to 6
- pivots: int32 [3, 384], replicated, may hold values from 0 to 6143, as said below
- lower_inv: float32 [3, 384, 384], replicated, may hold values from -0.3125 to 0.3125
- upper_inv: float32 [3, 384, 384], replicated, may hold values from -0.015625 to 0.015625
Outputs:
- factored: float32 [8, 16, 768, 384], P('prow', 'pcol')
Inputs may be any that keep to these rules, and one draw needn't show every extreme that they name: Within one step s the indices pivots[s, i] are distinct, and each equals s * 384 + i or lies between (s + 1) * 384 and 6143.
All inputs are finite; a program needn't handle non-finite values.
Results may differ from a plain program's by a relative error of at most 0.0002.
Values sent between devices are 32-bit elements; how exact they have to be, the bound alone decides.
No kernel may reach another device: no remote copies, remote signals or barrier semaphores. Data moves between devices by JAX's collectives and lax.ppermute only.
A program may use at most 64 MiB of HBM per device.

v0:
```python
import jax
import jax.numpy as jnp
from jax import lax
from jax.sharding import PartitionSpec as P

PRECISE = lax.Precision.HIGHEST


def over_pieces(x, axis):
    parts = lax.all_gather(x, axis)
    return parts.sum(axis=0)


def spread(value, axis, source):
    kept = jnp.where(lax.axis_index(axis) == source, value, 0).astype(value.dtype)
    return lax.psum(kept, axis)


def on_device(matrix, pivots, lower_inv, upper_inv):
    prow_count = lax.axis_size("prow")
    pcol_count = lax.axis_size("pcol")
    prow_index = lax.axis_index("prow")
    pcol_index = lax.axis_index("pcol")
    local_tile = matrix[0, 0]
    local_rows, local_cols = local_tile.shape
    width = lower_inv.shape[1]
    row_ids = jnp.arange(local_rows, dtype=jnp.int32)
    global_rows = (row_ids // width * prow_count + prow_index) * width + row_ids % width
    col_ids = jnp.arange(local_cols, dtype=jnp.int32)
    global_cols = (col_ids // width * pcol_count + pcol_index) * width + col_ids % width
    offsets = jnp.arange(width, dtype=jnp.int32)
    for section in range(pivots.shape[0]):
        start = section * width
        finish = start + width
        pivot_list = pivots[section]
        block_targets = start + offsets
        owner_row = section % prow_count
        owner_col = section % pcol_count
        row_start = section // prow_count * width
        targets = jnp.concatenate([block_targets, pivot_list])
        sources = jnp.concatenate([pivot_list, block_targets])
        source_owned = sources // width % prow_count == prow_index
        source_local = jnp.where(
            source_owned, sources // width // prow_count * width + sources % width, 0
        )
        picked = jnp.where(source_owned[:, None], local_tile[source_local], 0.0)
        arrived = over_pieces(picked, "prow")
        target_owned = targets // width % prow_count == prow_index
        target_local = jnp.where(
            target_owned, targets // width // prow_count * width + targets % width, local_rows
        )
        local_tile = local_tile.at[target_local].set(arrived, mode="drop")
        pivot_rows = arrived[:width]
        lower_unit = jnp.eye(width, dtype=jnp.float32) + jnp.tril(lower_inv[section], -1)
        upper_tri = jnp.triu(upper_inv[section])
        col_mask = (global_cols >= finish)[None, :]
        row_mask = (global_rows >= finish)[:, None]
        product = jnp.dot(
            lower_unit, pivot_rows, precision=PRECISE, preferred_element_type=jnp.float32
        )
        upper_rows = jnp.where(col_mask, product, 0.0)
        current = local_tile[row_start : row_start + width]
        stored = jnp.where(col_mask & (prow_index == owner_row), upper_rows, current)
        local_tile = local_tile.at[row_start : row_start + width].set(stored)
        col_start = section // pcol_count * width
        panel = local_tile

        def lower_product(source_panel):
            product = jnp.dot(
                source_panel, upper_tri, precision=PRECISE, preferred_element_type=jnp.float32
            )
            return jnp.where(row_mask, product, 0.0)

        def owned_lower():
            return lower_product(panel)

        def empty_panel():
            return jnp.zeros_like(panel)

        owned_panel = lax.cond(pcol_index == owner_col, owned_lower, empty_panel)
        lower_panel = spread(owned_panel, "pcol", owner_col)
        kept = jnp.where(row_mask & (pcol_index == owner_col), lower_panel, panel)
        local_tile = local_tile.at[:, col_start : col_start + width].set(kept)
        update = jnp.dot(
            lower_panel, upper_rows, precision=PRECISE, preferred_element_type=jnp.float32
        )
        local_tile = local_tile - update
    return local_tile[None, None]


def solution(mesh):
    return jax.shard_map(
        on_device,
        mesh=mesh,
        in_specs=(P("prow", "pcol", None, None), P(), P(), P()),
        out_specs=P("prow", "pcol", None, None),
        check_vma=False,
    )
```

profile of v0, /device:TPU:0, one launch (start us, length us, event | category | flops | bytes accessed | tf_op | source)
XLA Modules:
  0.0 510.7 jit_solution(8348842341577072828)
XLA Ops:
  6.5 1.3 copy.37
  8.6 2.1 gather_fusion
  12.9 55.8 %all-gather.4.cloned.1.call-done = f32[8,768,384]{2,1,0:T(8,128)} async-done(((f32[1,768,384]{2,1,0:T(8,128)}), f32[8,768,384]{2,1,0:T(8,128)}) %all-gather.4.cloned.1.call-update) | async-done | bytes 9437200 | tf_op jit(solution)/shard_map/all_gather | solution.py:10
  68.7 4.3 reduce_sum.27
  72.9 5.7 %scatter_fusion = f32[768,384]{1,0:T(8,128)S(1)} fusion(f32[768,384]{1,0:T(8,128)S(1)} %bitcast.61, s32[768]{0:T(1024)S(1)} %get-tuple-element.181, f32[768,384]{1,0:T(8,128)S(1)} %reduce_sum.27), kind=kCustom, calls=%fused_computation.3 | custom fusion | bytes 3542016 | tf_op jit(solution)/shard_map/scatter | solution.py:52
  78.6 3.5 fusion.17
  82.2 4.4 conditional.3
  82.2 4.0 fusion
  88.5 82.4 %all-reduce.4.cloned.1.call-done = f32[768,384]{1,0:T(8,128)} async-done(((f32[768,384]{1,0:T(8,128)}), f32[768,384]{1,0:T(8,128)}) %all-reduce.4.cloned.1.call-update) | async-done | bytes 1179664 | tf_op jit(solution)/shard_map/psum | solution.py:16
  170.8 4.0 convolution_subtract_fusion.2
  174.8 2.1 gather_fusion.1
  178.2 53.3 %all-gather.6.cloned.1.call-done = f32[8,768,384]{2,1,0:T(8,128)} async-done(((f32[1,768,384]{2,1,0:T(8,128)}), f32[8,768,384]{2,1,0:T(8,128)}) %all-gather.6.cloned.1.call-update) | async-done | bytes 9437200 | tf_op jit(solution)/shard_map/all_gather | solution.py:10
  231.5 4.3 reduce_sum.28
  235.8 5.7 %scatter_fusion.1 = f32[768,384]{1,0:T(8,128)S(1)} fusion(f32[768,384]{1,0:T(8,128)S(1)} %convolution_subtract_fusion.2, s32[768]{0:T(1024)S(1)} %get-tuple-element.179, f32[768,384]{1,0:T(8,128)S(1)} %reduce_sum.28), kind=kCustom, calls=%fused_computation.4 | custom fusion | bytes 3542016 | tf_op jit(solution)/shard_map/scatter | solution.py:52
  241.5 3.5 fusion.15
  247.0 86.9 %all-reduce.6.cloned.1.call-done = f32[768,384]{1,0:T(8,128)} async-done(((f32[768,384]{1,0:T(8,128)}), f32[768,384]{1,0:T(8,128)}) %all-reduce.6.cloned.1.call-update) | async-done | bytes 1179664 | tf_op jit(solution)/shard_map/psum | solution.py:16
  333.9 4.0 convolution_subtract_fusion.1
  337.9 2.1 gather_fusion.2
  341.3 53.3 %all-gather.8.cloned.1.call-done = f32[8,768,384]{2,1,0:T(8,128)} async-done(((f32[1,768,384]{2,1,0:T(8,128)}), f32[8,768,384]{2,1,0:T(8,128)}) %all-gather.8.cloned.1.call-update) | async-done | bytes 9437200 | tf_op jit(solution)/shard_map/all_gather | solution.py:10
  394.6 4.3 reduce_sum.29
  398.9 5.7 %scatter_fusion.2 = f32[768,384]{1,0:T(8,128)S(1)} fusion(f32[768,384]{1,0:T(8,128)S(1)} %convolution_subtract_fusion.1, s32[768]{0:T(1024)S(1)} %get-tuple-element.177, f32[768,384]{1,0:T(8,128)S(1)} %reduce_sum.29), kind=kCustom, calls=%fused_computation.5 | custom fusion | bytes 3542016 | tf_op jit(solution)/shard_map/scatter | solution.py:52
  404.6 3.5 fusion.13
  409.6 89.2 %all-reduce.8.cloned.1.call-done = f32[768,384]{1,0:T(8,128)} async-done(((f32[768,384]{1,0:T(8,128)}), f32[768,384]{1,0:T(8,128)}) %all-reduce.8.cloned.1.call-update) | async-done | bytes 1179664 | tf_op jit(solution)/shard_map/psum | solution.py:16
  498.8 5.0 fusion.12
  (69 shorter events, 11.2 us)
Async XLA Ops:
  6.5 1.3 copy-start.8
  6.5 62.1 %all-gather.4.cloned.1.call-start = ((), (), s32[]{:S(2)}) async-start(), calls=%async_computation | async-start | bytes 10616832 | tf_op jit(solution)/shard_map/all_gather | solution.py:10
  11.9 158.9 %all-reduce.4.cloned.1.call-start = ((), (), s32[]{:S(2)}) async-start(), calls=%async_computation.1 | async-start | bytes 2359296 | tf_op jit(solution)/shard_map/psum | solution.py:16
  78.6 3.5 copy-start
  87.7 0.7 copy-start.7
  87.7 83.2 %copy-start.3 = (f32[384,384]{1,0:T(8,128)S(1)}, f32[384,384]{1,0:T(8,128)}, u32[]{:S(2)}) copy-start(f32[384,384]{1,0:T(8,128)} %get-tuple-element.186) | copy-start | bytes 1769476
  87.7 143.8 %all-gather.6.cloned.1.call-start = ((), (), s32[]{:S(2)}) async-start(), calls=%async_computation.2 | async-start | bytes 10616832 | tf_op jit(solution)/shard_map/all_gather | solution.py:10
  178.2 155.8 %all-reduce.6.cloned.1.call-start = ((), (), s32[]{:S(2)}) async-start(), calls=%async_computation.3 | async-start | bytes 2359296 | tf_op jit(solution)/shard_map/psum | solution.py:16
  241.5 3.5 copy-start.1
  246.2 0.7 copy-start.6
  246.2 87.8 %copy-start.4 = (f32[384,384]{1,0:T(8,128)S(1)}, f32[384,384]{1,0:T(8,128)}, u32[]{:S(2)}) copy-start(f32[384,384]{1,0:T(8,128)} %get-tuple-element.188) | copy-start | bytes 1769476
  246.2 148.4 %all-gather.8.cloned.1.call-start = ((), (), s32[]{:S(2)}) async-start(), calls=%async_computation.4 | async-start | bytes 10616832 | tf_op jit(solution)/shard_map/all_gather | solution.py:10
  341.3 157.6 %all-reduce.8.cloned.1.call-start = ((), (), s32[]{:S(2)}) async-start(), calls=%async_computation.5 | async-start | bytes 2359296 | tf_op jit(solution)/shard_map/psum | solution.py:16
  404.6 3.5 copy-start.2
  409.5 89.3 %copy-start.5 = (f32[384,384]{1,0:T(8,128)S(1)}, f32[384,384]{1,0:T(8,128)}, u32[]{:S(2)}) copy-start(f32[384,384]{1,0:T(8,128)} %get-tuple-element.190) | copy-start | bytes 1769476
Sparse Core Ops, SparseCore 0:
  12.1 56.5 all-gather.3
  87.8 82.9 all-reduce.3
  178.3 53.1 all-gather.5
  246.3 87.5 all-reduce.5
  341.4 53.1 all-gather.7
  409.7 89.0 all-reduce.7
where the time goes:
time: 511 us
  waiting for transfers between devices  421 us (82%)
  matrix products  27.5 us (5%)
  local copies, waits for them, and re-layouts  26.7 us (5%)
  other arithmetic  20.9 us (4%)
  between operations  13.8 us (3%)
    psum x3, waiting for transfers between devices, spread(): return lax.psum(kept, axis)  259 us
    all_gather x3, waiting for transfers between devices, over_pieces(): parts = lax.all_gather(x, axis)  162 us
    scatter x3, local copies, waits for them, and re-layouts, on_device(): local_tile = local_tile.at[target_local].set(arrived, mode='drop')  17.1 us
    dot_general x3, matrix products, on_device(): jnp.dot(lower_panel, upper_rows, precision=PRECISE, preferred_element_typ...  12.9 us
    reduce_sum x3, other arithmetic, over_pieces(): return parts.sum(axis=0)  12.8 us
    dot_general x3, matrix products, on_device(): jnp.dot(lower_unit, pivot_rows, precision=PRECISE, preferred_element_type...  10.5 us
  transfers between devices with their start and end apart: 6, of which 6 were waited for; matrix products, arithmetic and copies ran while one was open for 0% of the time, Pallas kernels for 0%

commit v1 on v0

--- a/solution.py
+++ b/solution.py
@@ -13,7 +13,8 @@
 
 def spread(value, axis, source):
     kept = jnp.where(lax.axis_index(axis) == source, value, 0).astype(value.dtype)
-    return lax.psum(kept, axis)
+    draw_targets = lambda dev_axis, content: jnp.sum(jax.lax.all_gather(content, dev_axis), axis=0)
+    return draw_targets(axis, kept)
 
 
 def on_device(matrix, pivots, lower_inv, upper_inv):

time: 511 us -> 674 us (1.32); the launches traced: 511 us -> 666 us
  waiting for transfers between devices: 421 us -> 525 us
  local copies, waits for them, and re-layouts: 26.7 us -> 66.5 us
  other arithmetic: 20.9 us -> 32.1 us
    all_gather x0 -> x3, waiting for transfers between devices: none -> 361 us  [spread(): jax.lax.all_gather(content, dev_axis)]
    psum x3 -> x0, waiting for transfers between devices: 259 us -> none  [spread(): return lax.psum(kept, axis)]
    unnamed x19 -> x20, local copies, waits for them, and re-layouts: 2.07 us -> 38.2 us
    reduce_sum x0 -> x3, other arithmetic: none -> 9.63 us  [spread(): jnp.sum(jax.lax.all_gather(content, dev_axis), axis=0)]
where the time goes in v1:
time: 674 us; the launch traced here: 666 us
  waiting for transfers between devices  525 us (78%)
  local copies, waits for them, and re-layouts  66.5 us (10%)
  other arithmetic  32.1 us (5%)
  matrix products  26.5 us (4%)
  between operations  14.1 us (2%)
    all_gather x3, waiting for transfers between devices, spread(): jax.lax.all_gather(content, dev_axis)  361 us
    all_gather x3, waiting for transfers between devices, over_pieces(): parts = lax.all_gather(x, axis)  164 us
    unnamed x20, local copies, waits for them, and re-layouts  38.2 us
    scatter x3, local copies, waits for them, and re-layouts, on_device(): local_tile = local_tile.at[target_local].set(arrived, mode='drop')  17.3 us
  transfers between devices with their start and end apart: 6, of which 6 were waited for; matrix products, arithmetic and copies ran while one was open for 0% of the time, Pallas kernels for 0%

profile of v1, /device:TPU:0, one launch (start us, length us, event | category | flops | bytes accessed | tf_op | source)
XLA Modules:
  0.0 665.7 jit_solution(17857442303662967924)
XLA Ops:
  12.9 56.3 %all-gather.10.cloned.1.call-done = f32[8,768,384]{2,1,0:T(8,128)} async-done(((f32[1,768,384]{2,1,0:T(8,128)}), f32[8,768,384]{2,1,0:T(8,128)}) %all-gather.10.cloned.1.call-update) | async-done | bytes 9437200 | tf_op jit(solution)/shard_map/all_gather | solution.py:10
  69.2 4.3 reduce_sum.54
  73.5 5.7 scatter_fusion
  79.2 3.4 fusion.17
  82.7 4.1 conditional.3
  82.7 4.0 fusion
  89.6 116.8 %all-gather.16.cloned.1.call-done = f32[12288,384]{0,1:T(8,128)} async-done(((f32[768,384]{0,1:T(8,128)}), f32[12288,384]{0,1:T(8,128)}) %all-gather.16.cloned.1.call-update) | async-done | bytes 18874384 | tf_op jit(solution)/shard_map/all_gather | solution.py:16
  206.4 12.1 %copy.8 = f32[48,8,16,768]{3,2,1,0:T(8,128)S(1)} copy(f32[48,8,16,768]{3,1,2,0:T(8,128)} %bitcast.78) | data formatting | bytes 37748736
  218.6 3.2 bitcast_reduce_fusion.2
  223.2 3.8 convolution_subtract_fusion.2
  230.4 53.8 %all-gather.12.cloned.1.call-done = f32[8,768,384]{2,1,0:T(8,128)} async-done(((f32[1,768,384]{2,1,0:T(8,128)}), f32[8,768,384]{2,1,0:T(8,128)}) %all-gather.12.cloned.1.call-update) | async-done | bytes 9437200 | tf_op jit(solution)/shard_map/all_gather | solution.py:10
  284.2 4.3 reduce_sum.56
  288.5 5.7 scatter_fusion.1
  294.2 3.5 fusion.15
  300.9 120.7 %all-gather.18.cloned.1.call-done = f32[12288,384]{0,1:T(8,128)} async-done(((f32[768,384]{0,1:T(8,128)}), f32[12288,384]{0,1:T(8,128)}) %all-gather.18.cloned.1.call-update) | async-done | bytes 18874384 | tf_op jit(solution)/shard_map/all_gather | solution.py:16
  421.6 12.1 %copy.9 = f32[48,8,16,768]{3,2,1,0:T(8,128)S(1)} copy(f32[48,8,16,768]{3,1,2,0:T(8,128)} %bitcast.77) | data formatting | bytes 37748736
  438.3 3.8 convolution_subtract_fusion.1
  445.6 53.8 %all-gather.14.cloned.1.call-done = f32[8,768,384]{2,1,0:T(8,128)} async-done(((f32[1,768,384]{2,1,0:T(8,128)}), f32[8,768,384]{2,1,0:T(8,128)}) %all-gather.14.cloned.1.call-update) | async-done | bytes 9437200 | tf_op jit(solution)/shard_map/all_gather | solution.py:10
  499.4 4.3 reduce_sum.58
  503.6 5.9 scatter_fusion.2
  509.6 3.5 fusion.13
  514.5 123.9 %all-gather.20.cloned.1.call-done = f32[12288,384]{0,1:T(8,128)} async-done(((f32[768,384]{0,1:T(8,128)}), f32[12288,384]{0,1:T(8,128)}) %all-gather.20.cloned.1.call-update) | async-done | bytes 18874384 | tf_op jit(solution)/shard_map/all_gather | solution.py:16
  638.5 12.1 %copy.10 = f32[48,8,16,768]{3,2,1,0:T(8,128)S(1)} copy(f32[48,8,16,768]{3,1,2,0:T(8,128)} %bitcast.79) | data formatting | bytes 37748736
  654.2 4.5 fusion.12
  (75 shorter events, 30.4 us)
Async XLA Ops:
  6.5 1.3 copy-start.7
  6.5 62.7 %all-gather.10.cloned.1.call-start = ((), (), s32[]{:S(2)}) async-start(), calls=%async_computation | async-start | bytes 10616832 | tf_op jit(solution)/shard_map/all_gather | solution.py:10
  12.5 193.9 %all-gather.16.cloned.1.call-start = ((), (), s32[]{:S(2)}) async-start(), calls=%async_computation.3 | async-start | bytes 20054016 | tf_op jit(solution)/shard_map/all_gather | solution.py:16
  12.9 69.8 %copy-start = (pred[384,384]{1,0:T(32,128)(4,1)}, pred[384,384]{1,0:T(32,128)(4,1)S(1)}, u32[]{:S(2)}) copy-start(pred[384,384]{1,0:T(32,128)(4,1)S(1)} %iota_compare_fusion.4) | copy-start | bytes 442372
  87.8 196.3 %all-gather.12.cloned.1.call-start = ((), (), s32[]{:S(2)}) async-start(), calls=%async_computation.1 | async-start | bytes 10616832 | tf_op jit(solution)/shard_map/all_gather | solution.py:10
  227.0 2.2 copy-start.5
  230.3 191.3 %all-gather.18.cloned.1.call-start = ((), (), s32[]{:S(2)}) async-start(), calls=%async_computation.4 | async-start | bytes 20054016 | tf_op jit(solution)/shard_map/all_gather | solution.py:16
  294.2 3.5 copy-start.1
  299.0 0.7 copy-start.4
  299.0 1.3 copy-start.3
  299.1 200.3 %all-gather.14.cloned.1.call-start = ((), (), s32[]{:S(2)}) async-start(), calls=%async_computation.2 | async-start | bytes 10616832 | tf_op jit(solution)/shard_map/all_gather | solution.py:10
  442.1 2.2 copy-start.6
  445.5 192.9 %all-gather.20.cloned.1.call-start = ((), (), s32[]{:S(2)}) async-start(), calls=%async_computation.5 | async-start | bytes 20054016 | tf_op jit(solution)/shard_map/all_gather | solution.py:16
  509.6 3.5 copy-start.2
Sparse Core Ops, SparseCore 0:
  12.7 56.5 all-gather.9
  88.0 118.4 all-gather.15
  230.5 53.6 all-gather.11
  299.2 122.3 all-gather.17
  445.6 53.6 all-gather.13
  514.6 123.7 all-gather.19
